TPU v7x, 128 devices: a whole 4x4x4 slice. The times are simulated.
128 devices in a mesh: dp: 8 (over x, core), group: 16 (over z, y).
Axes of the slice: x: 4, y: 4, z: 4, core: 2. Of those that a mesh axis runs over, the one named last changes fastest.
Arguments:
- queries: float32 [49152, 1024], P(('dp', 'group')), parts along dimension 0, may hold values from -8 to 8
- passages: float32 [49152, 1024], P(('dp', 'group')), parts along dimension 0, may hold values from -8 to 8
- positives: int32 [49152], P(('dp', 'group')), parts along dimension 0, may hold values from 0 to 6143, each once
- weights: float32 [49152], P(('dp', 'group')), parts along dimension 0, may hold values from 1 to 16
Outputs:
- losses: float32 [49152], P(('dp', 'group')), parts along dimension 0
- grad_queries: float32 [49152, 1024], P(('dp', 'group')), parts along dimension 0
- grad_passages: float32 [49152, 1024], P(('dp', 'group')), parts along dimension 0
There are 8 independent parts, one for each index of `dp`. A program takes and returns all parts, laid end to end along the dimension named above; each array names one. Nothing has to cross between parts.
Inputs may be any that keep to these rules, and one draw needn't show every extreme that they name: `positives`: each of the 6144 passages is the positive of exactly one query.
All inputs are finite; a program needn't handle non-finite values.
Results may differ from a plain program's by a relative error of at most 0.011.
Values may be sent and summed in bfloat16 or wider, within the bound.
A program may use at most 128 MiB of HBM per device.

v0:
```python
import math

import jax
import jax.numpy as jnp
from jax import lax
from jax.sharding import PartitionSpec as P


def per_device(queries, passages, positives, weights):
    feat_width = queries.shape[1]
    inv_temp = 2.0 / math.sqrt(feat_width)
    query_half = queries.astype(jnp.bfloat16)
    passage_half = passages.astype(jnp.bfloat16)
    gathered = lax.all_gather(passage_half, "group", axis=0, tiled=True)
    scores = (
        lax.dot_general(
            query_half, gathered, (((1,), (1,)), ((), ())), preferred_element_type=jnp.float32
        )
        * inv_temp
    )
    row_max = jnp.max(scores, axis=1)
    log_total = row_max + jnp.log(jnp.sum(jnp.exp(scores - row_max[:, None]), axis=1))
    columns = jnp.arange(gathered.shape[0], dtype=jnp.int32)
    is_positive = columns[None, :] == positives[:, None]
    positive_score = jnp.sum(jnp.where(is_positive, scores, 0.0), axis=1)
    losses = log_total - positive_score
    row_weight = weights * inv_temp
    coefficient = (
        row_weight[:, None]
        * (jnp.exp(scores - log_total[:, None]) - is_positive.astype(jnp.float32))
    ).astype(jnp.bfloat16)
    grad_queries = jnp.dot(coefficient, gathered, preferred_element_type=jnp.float32)
    grad_passages = lax.psum_scatter(
        lax.dot_general(
            coefficient, query_half, (((0,), (0,)), ((), ())), preferred_element_type=jnp.float32
        ),
        "group",
        scatter_dimension=0,
        tiled=True,
    )
    return (losses, grad_queries, grad_passages)


def solution(mesh):
    placed = (
        P(("dp", "group"), None),
        P(("dp", "group"), None),
        P(("dp", "group")),
        P(("dp", "group")),
    )
    return jax.shard_map(
        per_device,
        mesh=mesh,
        in_specs=placed,
        out_specs=(P(("dp", "group")), P(("dp", "group"), None), P(("dp", "group"), None)),
        check_vma=False,
    )
```

profile of v0, /device:TPU:1, one launch (start us, length us, event | category | flops | bytes accessed | tf_op | source)
XLA Modules:
  0.0 289.3 jit_solution(18209151257851408576)
XLA Ops:
  7.2 0.0 all-gather.2.cloned.1.call-start
  7.2 2.4 convert_element_type.13
  9.6 0.0 all-gather.2.cloned.1.call-update
  9.6 0.0 reduce-scatter.2.cloned.1.call-start
  9.7 0.7 broadcast_multiply_fusion
  10.4 0.0 copy-start.2
  10.4 93.7 %all-gather.2.cloned.1.call-done = bf16[6144,1024]{1,0:T(8,128)(2,1)} async-done(((bf16[384,1024]{1,0:T(8,128)(2,1)}), bf16[6144,1024]{1,0:T(8,128)(2,1)}) %all-gather.2.cloned.1.call-update) | async-done | bytes 12582928 | tf_op jit(solution)/shard_map/all_gather | solution.py:14
  104.1 8.7 %fusion.5 = (f32[384]{0:T(512)S(1)}, f32[384,6144]{1,0:T(8,128)S(1)}) fusion(bf16[6144,1024]{1,0:T(8,128)(2,1)} %all-gather.2.cloned.1.call-done, f32[384,1024]{1,0:T(8,128)} %param.4), kind=kOutput, calls=%fused_computation.12 | convolution fusion | flops 4836949504 | bytes 23594496 | tf_op jit(solution)/shard_map/dot_general | solution.py:16
  112.8 0.0 copy-start
  112.8 0.0 copy-start.1
  112.8 0.0 copy-done.2
  112.8 2.9 %select_reduce_fusion = (f32[384]{0:T(512)S(1)}, f32[384]{0:T(512)S(1)}) fusion(f32[384,6144]{1,0:T(8,128)S(1)} %get-tuple-element.8, s32[384]{0:T(512)S(1)} %copy-done.2, f32[384]{0:T(512)S(1)} %get-tuple-element.7), kind=kLoop, calls=%fused_computation.1 | loop fusion | flops 11795712 | bytes 9443328 | tf_op jit(solution)/shard_map/reduce_sum | solution.py:25
  115.8 0.7 fusion.4
  116.5 0.0 copy-done
  116.5 0.0 copy-done.1
  116.5 12.8 %fusion = f32[6144,1024]{1,0:T(8,128)} fusion(f32[384,1024]{1,0:T(8,128)S(1)} %copy-done.1, f32[384,6144]{1,0:T(8,128)S(1)} %get-tuple-element.8, f32[384]{0:T(512)S(1)} %get-tuple-element.6, f32[384]{0:T(512)S(1)} %broadcast_multiply_fusion, s32[384]{0:T(512)S(1)} %copy-done.2), kind=kOutput, calls=%fused_computation.5 | convolution fusion | flops 4846387200 | bytes 36180480 | tf_op jit(solution)/shard_map/dot_general | solution.py:34
  129.3 0.0 reduce-scatter.2.cloned.1.call-update
  129.4 13.0 %fusion.3 = f32[384,1024]{1,0:T(8,128)} fusion(bf16[6144,1024]{1,0:T(8,128)(2,1)} %all-gather.2.cloned.1.call-done, f32[384,6144]{1,0:T(8,128)} %copy-done, f32[384]{0:T(512)S(1)} %get-tuple-element.6, f32[384]{0:T(512)S(1)} %broadcast_multiply_fusion, s32[384]{0:T(512)S(1)} %copy-done.2), kind=kOutput, calls=%fused_computation.10 | convolution fusion | flops 4845993984 | bytes 23597568 | tf_op jit(solution)/shard_map/dot_general | solution.py:32
  142.3 140.1 %reduce-scatter.2.cloned.1.call-done = f32[384,1024]{1,0:T(8,128)} async-done(((f32[6144,1024]{1,0:T(8,128)}), f32[384,1024]{1,0:T(8,128)}) %reduce-scatter.2.cloned.1.call-update) | async-done | bytes 1572880 | tf_op jit(solution)/shard_map/reduce_scatter | solution.py:33
Async XLA Ops:
  7.2 96.9 %all-gather.2.cloned.1.call-start = ((), (), s32[]{:S(2)}) async-start(), calls=%async_computation.1 | async-start | bytes 13369344 | tf_op jit(solution)/shard_map/all_gather | solution.py:14
  9.6 272.8 %reduce-scatter.2.cloned.1.call-start = ((), (), s32[]{:S(2)}) async-start(), calls=%async_computation.2 | async-start | bytes 26738688 | tf_op jit(solution)/shard_map/reduce_scatter | solution.py:33
  10.4 102.4 %copy-start.2 = (s32[384]{0:T(512)S(1)}, s32[384]{0:T(512)}, u32[]{:S(2)}) copy-start(s32[384]{0:T(512)} %param.6) | copy-start | bytes 4612
  112.8 3.7 %copy-start = (f32[384,6144]{1,0:T(8,128)}, f32[384,6144]{1,0:T(8,128)S(1)}, u32[]{:S(2)}) copy-start(f32[384,6144]{1,0:T(8,128)S(1)} %get-tuple-element.8) | copy-start | bytes 28311556
  112.8 3.7 %copy-start.1 = (f32[384,1024]{1,0:T(8,128)S(1)}, f32[384,1024]{1,0:T(8,128)}, u32[]{:S(2)}) copy-start(f32[384,1024]{1,0:T(8,128)} %param.4) | copy-start | bytes 4718596
Sparse Core Ops, SparseCore 0:
  10.7 93.3 all-gather.1
  129.5 152.8 reduce-scatter.1
where the time goes:
time: 289 us
  waiting for transfers between devices  234 us (81%)
  matrix products  34.5 us (12%)
  between operations  14.1 us (5%)
  other arithmetic  6.74 us (2%)
    reduce_scatter x1, waiting for transfers between devices, per_device(): lax.psum_scatter(lax.dot_general(coefficient, query_half, (((0,), (0,)),...  140 us
    all_gather x1, waiting for transfers between devices, per_device(): gathered = lax.all_gather(passage_half, 'group', axis=0, tiled=True)  93.7 us
    dot_general x1, matrix products, per_device(): jnp.dot(coefficient, gathered, preferred_element_type=jnp.float32)  13 us
    dot_general x1, matrix products, per_device(): lax.dot_general(coefficient, query_half, (((0,), (0,)), ((), ())), prefer...  12.8 us
    dot_general x1, matrix products, per_device(): lax.dot_general(query_half, gathered, (((1,), (1,)), ((), ())), preferred...  8.69 us
  transfers between devices with their start and end apart: 2, of which 2 were waited for; matrix products, arithmetic and copies ran while one was open for 5% of the time, Pallas kernels for 0%

commit v1 on v0

v1 whole, which is shorter than its diff:
```python
import functools
import math

import jax
import jax.numpy as jnp
from jax import lax
from jax.experimental import pallas as pl
from jax.experimental.pallas import tpu as pltpu
from jax.sharding import PartitionSpec as P

MESH = pl.DeviceIdType.MESH
SIDE = 4
OWN, NEXT, PREV, FAR = range(4)
STEP = (0, 1, 3, 2)
SEEN = tuple(tuple(STEP.index((STEP[s] + STEP[k]) % SIDE) for k in range(SIDE)) for s in range(SIDE))
LOG2E = math.log2(math.e)
BF16, F32 = jnp.bfloat16, jnp.float32


def kernel(
    rows, width, inv_temp,
    q_hbm, p_hbm, pos_ref, w_ref,
    loss_ref, gq_ref, gp_ref,
    stage, gathered, scores, coef, coef_t, meta, pos_all, stats, peak, shift, partial, sent, hop1, hop2,
    load_sem, ag_send, ag_recv, meta_send, meta_recv, st_send, st_recv, rs_send, rs_recv, go_sem,
):
    half, quarter = rows // 2, rows // 4
    total = SIDE * rows
    rate = inv_temp * LOG2E
    dp, me = lax.axis_index("dp"), lax.axis_index("group")
    z, y = me // SIDE, me % SIDE
    first = dp % 2 == 0
    sibling = dp + 1 - 2 * (dp % 2)

    def at(axis, slot):
        if axis == 0:
            return (dp, z * SIDE + (y + STEP[slot]) % SIDE)
        return (dp, (z + STEP[slot]) % SIDE * SIDE + y)

    greet = [at(0, NEXT), at(0, PREV), at(0, FAR), at(1, NEXT), at(1, PREV), (sibling, me)]
    barrier = pltpu.get_barrier_semaphore()
    for device in greet:
        pl.semaphore_signal(barrier, inc=1, device_id=device, device_id_type=MESH)

    loads = [pltpu.make_async_copy((q_hbm, p_hbm)[a], stage.at[a], load_sem.at[a]) for a in range(2)]
    for load in loads:
        load.start()
    meta[OWN] = jnp.zeros(meta.shape[1:], F32)
    meta[OWN, 0:1, :] = pos_ref[...].astype(F32)
    meta[OWN, 1:2, :] = w_ref[...]

    for a in range(2):
        loads[a].wait()

        @pl.loop(0, rows // 64)
        def _(i):
            part = pl.ds(pl.multiple_of(i * 64, 64), 64)
            gathered[a, part, :] = stage[a, part, :].astype(BF16)

    pl.semaphore_wait(barrier, len(greet))

    @pl.when(jnp.logical_not(first))
    def _():
        pl.semaphore_wait(go_sem, 1)

    def block(slot, h=None):
        if h is None:
            return pl.ds(slot * rows, rows)
        return pl.ds(slot * rows + h * half, half)

    def remote(src, dst, send, recv, device):
        return pltpu.make_async_remote_copy(
            src_ref=src, dst_ref=dst, send_sem=send, recv_sem=recv, device_id=device, device_id_type=MESH
        )

    metas = [
        remote(meta.at[OWN], meta.at[STEP.index(-STEP[s] % SIDE)], meta_send.at[s], meta_recv.at[s], at(0, s))
        for s in (NEXT, PREV, FAR)
    ]
    for copy in metas:
        copy.start()

    def ag(a, d, k):
        h = (0, 1, 0)[k] if d == 0 else (1, 0, 1)[k]
        near = (NEXT, PREV)[d]
        src, dst = (OWN, near) if k < 2 else (near, FAR)
        return remote(
            gathered.at[a, block(src, h)], gathered.at[a, block(dst, h)],
            ag_send.at[a, d, k], ag_recv.at[a, d, k], at(a, (PREV, NEXT)[d]),
        )

    pairs = [(a, d) for d in range(2) for a in (1, 0)]
    for k in range(2):
        for a, d in pairs:
            ag(a, d, k).start()

    peak[...] = jnp.full(peak.shape, -jnp.inf, F32)

    def score(j, i0, cols):
        part = pl.ds(pl.multiple_of(j * quarter, quarter), quarter)
        r = lax.dot_general(
            gathered[1, part, :], gathered[0, i0 : i0 + cols, :], (((1,), (1,)), ((), ())),
            preferred_element_type=F32,
        )
        scores[part, i0 : i0 + cols] = r
        top = jnp.max(r.reshape(quarter // 8, 8, cols), axis=0)
        peak[:, i0 : i0 + cols] = jnp.maximum(peak[:, i0 : i0 + cols], top)

    @pl.loop(0, 4)
    def _(j):
        score(j, 0, rows)

    for a, d in pairs:
        ag(a, d, 0).wait_recv()
        ag(a, d, 2).start()
    for a, d in pairs:
        ag(a, d, 0).wait_send()
        ag(a, d, 1).wait_send()

    @pl.when(first)
    def _():
        pl.semaphore_signal(go_sem, inc=1, device_id=(sibling, me), device_id_type=MESH)

    for a, d in pairs:
        ag(a, d, 1).wait_recv()

    @pl.loop(0, 4)
    def _(j):
        score(j, rows, 2 * rows)

    @pl.loop(4, 12)
    def _(j):
        score(j, 0, 3 * rows)

    for copy in metas:
        copy.wait()
    for s in range(SIDE):
        pos_all[:, block(s)] = jnp.broadcast_to(meta[s, 0:1, :], (8, rows)).astype(jnp.int32)

    for a, d in pairs:
        ag(a, d, 2).wait_recv()

    @pl.loop(0, 12)
    def _(j):
        score(j, 3 * rows, rows)

    @pl.loop(12, 16)
    def _(j):
        score(j, 0, total)

    top = jnp.max(peak[...], axis=0, keepdims=True)
    shift[0:1, :] = top
    zero = jnp.zeros((8, total), F32)
    strip = 16
    wide = rows
    peak[...] = zero
    shift[8:16, :] = zero

    def base(slot):
        owner = (z + STEP[slot]) % SIDE * SIDE + y
        return owner * rows

    for s in range(SIDE):

        @pl.loop(0, rows // strip)
        def _(i):
            part = pl.ds(pl.multiple_of(s * rows + i * strip, strip), strip)
            for c in range(0, total, wide):
                cols = pl.ds(c, wide)
                r = scores[part, cols]
                e = jnp.exp2((r - shift[0:1, cols]) * rate)
                hit = lax.broadcasted_iota(jnp.int32, (strip, wide), 0) == pos_all[0:1, cols] - (base(s) + i * strip)
                g = jnp.where(hit, r, 0.0)
                peak[:, cols] += jnp.sum(e.reshape(strip // 8, 8, wide), axis=0)
                shift[8:16, cols] += jnp.sum(g.reshape(strip // 8, 8, wide), axis=0)

    for s in range(SIDE):
        cols = block(s)
        stats[OWN, s] = jnp.zeros(stats.shape[2:], F32)
        stats[OWN, s, 0:1, :] = shift[0:1, cols]
        stats[OWN, s, 1:2, :] = jnp.sum(peak[:, cols], axis=0, keepdims=True)
        stats[OWN, s, 2:3, :] = jnp.sum(shift[8:16, cols], axis=0, keepdims=True)
    posts = [
        remote(stats.at[OWN], stats.at[STEP.index(-STEP[s] % SIDE)], st_send.at[s], st_recv.at[s], at(0, s))
        for s in (NEXT, PREV, FAR)
    ]
    for copy in posts:
        copy.start()
    for copy in posts:
        copy.wait()
    for k in range(SIDE):
        mine = [stats[s, SEEN[s].index(k)] for s in range(SIDE)]
        top = functools.reduce(jnp.maximum, [m[0:1] for m in mine])
        mass = sum(m[1:2] * jnp.exp2((m[0:1] - top) * rate) for m in mine)
        scale = meta[k, 1:2, :] * inv_temp
        shift[0:1, block(k)] = top + (jnp.log2(mass) - jnp.log2(scale)) * (1.0 / rate)
        shift[1:2, block(k)] = scale
        if k == OWN:
            hit = sum(m[2:3] for m in mine)
            loss_ref[...] = (top - hit) * inv_temp + jnp.log(mass)

    def coefficients(s, i0, cols):
        @pl.loop(0, rows // strip)
        def _(i):
            part = pl.ds(pl.multiple_of(s * rows + i * strip, strip), strip)
            for c in range(i0, i0 + cols, wide):
                lanes = pl.ds(c, wide)
                e = jnp.exp2((scores[part, lanes] - shift[0:1, lanes]) * rate)
                hit = lax.broadcasted_iota(jnp.int32, (strip, wide), 0) == pos_all[0:1, lanes] - (base(s) + i * strip)
                coef[part, lanes] = (e - jnp.where(hit, shift[1:2, lanes], 0.0)).astype(BF16)

    def turn(k):
        @pl.loop(0, SIDE)
        def _(s):
            part = pl.ds(pl.multiple_of(s * rows, rows), rows)
            coef_t[k * rows : (k + 1) * rows, part] = coef[part, k * rows : (k + 1) * rows].T

    tile = min(width, 256)

    def product(a, k, put):
        @pl.loop(0, width // tile)
        def _(n):
            cols = pl.ds(pl.multiple_of(n * tile, tile), tile)
            lhs = coef_t if a == 0 else coef
            r = jnp.dot(
                lhs[k * rows : (k + 1) * rows, :], gathered[1 - a, :, cols], preferred_element_type=F32
            )
            put(r, cols)

    def rs(a, d, k):
        h = (d, d, 1 - d, d, d)[k]
        if k < 2:
            rows_of = pl.ds(h * half + k * quarter, quarter)
            src, dst = sent.at[a, 2, rows_of], hop1.at[a, d, pl.ds(k * quarter, quarter)]
        elif k == 2:
            rows_of = pl.ds(h * half, half)
            src, dst = sent.at[a, d, rows_of], hop2.at[a, d, rows_of]
        else:
            rows_of = pl.ds(h * half + (k - 3) * quarter, quarter)
            src, dst = sent.at[a, d, rows_of], hop2.at[a, d, rows_of]
        return remote(src, dst, rs_send.at[a, d, k], rs_recv.at[a, d, k], at(a, (PREV, NEXT)[d]))

    def far(a):
        def put(r, cols):
            sent[a, 2, :, cols] = r.astype(BF16)

        product(a, FAR, put)
        for k in range(2):
            for d in range(2):
                rs(a, d, k).start()

    def near(a, d):
        def put(r, cols):
            keep = r[half:, :] if d == 1 else r[:half, :]
            send = r[:half, :] if d == 1 else r[half:, :]
            partial[a, d, :, cols] = keep
            sent[a, d, (1 - d) * half : (2 - d) * half, cols] = send.astype(BF16)

        product(a, (PREV, NEXT)[d], put)
        rs(a, d, 2).start()

    def own(a):
        out = (gq_ref, gp_ref)[a]

        def put(r, cols):
            out[:, cols] = r

        product(a, OWN, put)

    def pass_on(a, d, k):
        rs(a, d, k).wait_recv()
        rows_of = slice(d * half + k * quarter, d * half + (k + 1) * quarter)
        sent[a, d, rows_of, :] = (
            partial[a, d, k * quarter : (k + 1) * quarter, :]
            + hop1[a, d, k * quarter : (k + 1) * quarter, :].astype(F32)
        ).astype(BF16)
        rs(a, d, k + 3).start()

    coefficients(FAR, 0, total)
    far(1)
    for s in (OWN, NEXT, PREV):
        coefficients(s, 3 * rows, rows)
    turn(FAR)
    far(0)
    for s in (NEXT, PREV, OWN):
        coefficients(s, 0, 3 * rows)
    for d in range(2):
        near(1, d)
    turn(PREV)
    near(0, 0)
    turn(NEXT)
    near(0, 1)
    for k in range(2):
        for a in (1, 0):
            for d in range(2):
                pass_on(a, d, k)
    turn(OWN)
    own(1)
    own(0)

    def add(a, d, k):
        rs(a, d, k).wait_recv()
        out = (gq_ref, gp_ref)[a]
        h = (d, d, 1 - d, d, d)[k]
        start, size = (h * half, half) if k == 2 else (h * half + (k - 3) * quarter, quarter)
        out[start : start + size, :] += hop2[a, d, start : start + size, :].astype(F32)

    for k in (2, 3, 4):
        for a in (1, 0):
            for d in range(2):
                add(a, d, k)

    for a, d in pairs:
        ag(a, d, 2).wait_send()
        for k in range(5):
            rs(a, d, k).wait_send()


def per_device(queries, passages, positives, weights):
    rows, width = queries.shape
    total = SIDE * rows
    inv_temp = 2.0 / math.sqrt(width)
    vmem = pl.BlockSpec(memory_space=pltpu.VMEM)
    hbm = pl.BlockSpec(memory_space=pl.ANY)
    dma = pltpu.SemaphoreType.DMA
    losses, grad_queries, grad_passages = pl.pallas_call(
        functools.partial(kernel, rows, width, inv_temp),
        out_shape=(
            jax.ShapeDtypeStruct((1, rows), F32),
            jax.ShapeDtypeStruct((rows, width), F32),
            jax.ShapeDtypeStruct((rows, width), F32),
        ),
        in_specs=[hbm, hbm, vmem, vmem],
        out_specs=(vmem, vmem, vmem),
        scratch_shapes=[
            pltpu.VMEM((2, rows, width), F32),
            pltpu.VMEM((2, total, width), BF16),
            pltpu.VMEM((total, total), F32),
            pltpu.VMEM((total, total), BF16),
            pltpu.VMEM((total, total), BF16),
            pltpu.VMEM((SIDE, 8, rows), F32),
            pltpu.VMEM((8, total), jnp.int32),
            pltpu.VMEM((SIDE, SIDE, 8, rows), F32),
            pltpu.VMEM((8, total), F32),
            pltpu.VMEM((16, total), F32),
            pltpu.VMEM((2, 2, rows // 2, width), F32),
            pltpu.VMEM((2, 3, rows, width), BF16),
            pltpu.VMEM((2, 2, rows // 2, width), BF16),
            pltpu.VMEM((2, 2, rows, width), BF16),
            dma((2,)),
            dma((2, 2, 3)),
            dma((2, 2, 3)),
            dma((SIDE,)),
            dma((SIDE,)),
            dma((SIDE,)),
            dma((SIDE,)),
            dma((2, 2, 5)),
            dma((2, 2, 5)),
            pltpu.SemaphoreType.REGULAR,
        ],
        compiler_params=pltpu.CompilerParams(
            collective_id=0, has_side_effects=True, vmem_limit_bytes=60 * 2**20
        ),
    )(queries, passages, positives.reshape(1, rows), weights.reshape(1, rows))
    return losses.reshape(rows), grad_queries, grad_passages


def solution(mesh):
    split = P(("dp", "group"))
    whole = P(("dp", "group"), None)
    return jax.shard_map(
        per_device,
        mesh=mesh,
        in_specs=(whole, whole, split, split),
        out_specs=(split, whole, whole),
        check_vma=False,
    )
```

time: 289 us -> 97.4 us (0.34)
  waiting for transfers between devices: 234 us -> 0 us
  Pallas kernels: 0 us -> 88.8 us
  matrix products: 34.5 us -> 0 us
  between operations: 14.1 us -> 0.64 us
  local copies, waits for them, and re-layouts: 0.03 us -> 6.48 us
  other arithmetic: 6.74 us -> 1.27 us
    reduce_scatter x1 -> x0, waiting for transfers between devices: 140 us -> none  [per_device(): lax.psum_scatter(lax.dot_general(coefficient, query_half, (((0,), (0,)),...]
    all_gather x1 -> x0, waiting for transfers between devices: 93.7 us -> none  [per_device(): gathered = lax.all_gather(passage_half, 'group', axis=0, tiled=True)]
    pallas_call x0 -> x1, Pallas kernels: none -> 88.8 us  [per_device(): pl.pallas_call(functools.partial(kernel, rows, width, inv_temp), out_shap...]
    dot_general x3 -> x0, matrix products: 34.5 us -> none  [the longest x1 13 us: per_device(): jnp.dot(coefficient, gathered, preferred_element_type=jnp.float32)]
    unnamed x6 -> x4, local copies, waits for them, and re-layouts: 0.03 us -> 3.99 us
    reduce_sum x1 -> x0, other arithmetic: 2.94 us -> none  [per_device(): positive_score = jnp.sum(jnp.where(is_positive, scores, 0.0), axis=1)]
  transfers between devices with their start and end apart: 2 -> 0, of which waited for: 2 -> 0; matrix products, arithmetic and copies ran while one was open for 5% -> 0% of each run, Pallas kernels for 0% -> 0%
where the time goes in v1:
time: 97.4 us; the launch traced here: 97.2 us
  Pallas kernels  88.8 us (91%)
  local copies, waits for them, and re-layouts  6.48 us (7%)
  other arithmetic  1.27 us (1%)
    pallas_call x1, Pallas kernels, per_device(): pl.pallas_call(functools.partial(kernel, rows, width, inv_temp), out_shap...  88.8 us
    unnamed x4, local copies, waits for them, and re-layouts  3.99 us

profile of v1, /device:TPU:1, one launch (start us, length us, event | category | flops | bytes accessed | tf_op | source)
XLA Modules:
  0.0 97.2 jit_solution(7464769003027991761)
XLA Ops:
  0.6 1.2 %reshape.15.pos_ref = s32[1,384]{1,0:T(1,128)} reshape(s32[384]{0:T(512)} %param.6) | data formatting | bytes 3072 | tf_op jit(solution)/shard_map/reshape | solution.py:364
  1.9 1.2 %reshape.16.w_ref = f32[1,384]{1,0:T(1,128)} reshape(f32[384]{0:T(512)} %param.7) | data formatting | bytes 3072 | tf_op jit(solution)/shard_map/reshape | solution.py:364
  3.1 88.8 %shard_map.67 = (f32[1,384]{1,0:T(1,128)}, f32[384,1024]{1,0:T(8,128)}, f32[384,1024]{1,0:T(8,128)}) custom-call(f32[384,1024]{1,0:T(8,128)} %q_hbm.1, f32[384,1024]{1,0:T(8,128)} %p_hbm.1, s32[1,384]{1,0:T(1,128)} %reshape.15.pos_ref, f32[1,384]{1,0:T(1,128)} %reshape.16.w_ref), custom_call_target="tpu_custom_call" | custom-call | tf_op jit(solution)/shard_map/pallas_call | solution.py:326
  91.9 1.3 %reduce = f32[384]{0:T(512)} reduce(f32[1,384]{1,0:T(1,128)} %get-tuple-element.6, f32[]{:T(128)} %constant), dimensions={0}, to_apply=%get-tuple-element.6.reduce_sub_computation | reduce | bytes 3076 | tf_op jit(solution)/shard_map/pallas_call | solution.py:326
  93.2 0.0 copy-start
  93.2 2.8 %copy.9 = f32[384,1024]{1,0:T(8,128)} copy(f32[384,1024]{1,0:T(8,128)} %get-tuple-element.13) | data formatting | bytes 3145728
  96.0 0.0 copy-done
  96.0 1.1 %copy.10 = f32[384,1024]{1,0:T(8,128)} copy(f32[384,1024]{1,0:T(8,128)S(1)} %copy-done) | data formatting | bytes 3145728
Async XLA Ops:
  93.2 2.9 %copy-start = (f32[384,1024]{1,0:T(8,128)S(1)}, f32[384,1024]{1,0:T(8,128)}, u32[]{:S(2)}) copy-start(f32[384,1024]{1,0:T(8,128)} %get-tuple-element.14) | copy-start | bytes 4718596

commit v2 on v1

v2 whole, which is shorter than its diff:
```python
import functools
import math

import jax
import jax.numpy as jnp
from jax import lax
from jax.experimental import pallas as pl
from jax.experimental.pallas import tpu as pltpu
from jax.sharding import PartitionSpec as P

MESH = pl.DeviceIdType.MESH
SIDE = 4
OWN, NEXT, PREV, FAR = range(4)
STEP = (0, 1, 3, 2)
SEEN = tuple(tuple(STEP.index((STEP[s] + STEP[k]) % SIDE) for k in range(SIDE)) for s in range(SIDE))
LOG2E = math.log2(math.e)
BF16, F32 = jnp.bfloat16, jnp.float32


def kernel(
    rows, width, inv_temp,
    q_hbm, p_hbm, pos_ref, w_ref,
    loss_ref, gq_ref, gp_ref,
    stage, gathered, scores, coef, coef_t, meta, pos_all, stats, peak, mass, found, shift, partial, sent, hop1, hop2,
    load_sem, ag_send, ag_recv, meta_send, meta_recv, st_send, st_recv, rs_send, rs_recv, go_sem,
):
    half, quarter = rows // 2, rows // 4
    total = SIDE * rows
    rate = inv_temp * LOG2E
    dp, me = lax.axis_index("dp"), lax.axis_index("group")
    z, y = me // SIDE, me % SIDE
    first = dp % 2 == 0
    sibling = dp + 1 - 2 * (dp % 2)

    def at(axis, slot):
        if axis == 0:
            return (dp, z * SIDE + (y + STEP[slot]) % SIDE)
        return (dp, (z + STEP[slot]) % SIDE * SIDE + y)

    greet = [at(0, NEXT), at(0, PREV), at(0, FAR), at(1, NEXT), at(1, PREV), (sibling, me)]
    barrier = pltpu.get_barrier_semaphore()
    for device in greet:
        pl.semaphore_signal(barrier, inc=1, device_id=device, device_id_type=MESH)

    loads = [pltpu.make_async_copy((q_hbm, p_hbm)[a], stage.at[a], load_sem.at[a]) for a in range(2)]
    for load in loads:
        load.start()
    meta[OWN] = jnp.zeros(meta.shape[1:], F32)
    meta[OWN, 0:1, :] = pos_ref[...].reshape(1, rows).astype(F32)
    meta[OWN, 1:2, :] = w_ref[...].reshape(1, rows)

    for a in range(2):
        loads[a].wait()

        @pl.loop(0, rows // 64)
        def _(i):
            part = pl.ds(pl.multiple_of(i * 64, 64), 64)
            gathered[a, part, :] = stage[a, part, :].astype(BF16)

    pl.semaphore_wait(barrier, len(greet))

    @pl.when(jnp.logical_not(first))
    def _():
        pl.semaphore_wait(go_sem, 1)

    def block(slot, h=None):
        if h is None:
            return pl.ds(slot * rows, rows)
        return pl.ds(slot * rows + h * half, half)

    def remote(src, dst, send, recv, device):
        return pltpu.make_async_remote_copy(
            src_ref=src, dst_ref=dst, send_sem=send, recv_sem=recv, device_id=device, device_id_type=MESH
        )

    metas = [
        remote(meta.at[OWN], meta.at[STEP.index(-STEP[s] % SIDE)], meta_send.at[s], meta_recv.at[s], at(0, s))
        for s in (NEXT, PREV, FAR)
    ]
    for copy in metas:
        copy.start()

    def ag(a, d, k):
        near = (NEXT, PREV)[d]
        if k < 2:
            h = (k, 1 - k)[d]
            src, dst = block(OWN, h), block(near, h)
        else:
            start, size = d * half + (k - 2) * quarter, quarter
            src, dst = pl.ds(near * rows + start, size), pl.ds(FAR * rows + start, size)
        return remote(
            gathered.at[a, src], gathered.at[a, dst],
            ag_send.at[a, d, k], ag_recv.at[a, d, k], at(a, (PREV, NEXT)[d]),
        )

    pairs = [(a, d) for d in range(2) for a in (1, 0)]
    for k in range(2):
        for a, d in pairs:
            ag(a, d, k).start()

    def base(slot):
        owner = (z + STEP[slot]) % SIDE * SIDE + y
        return owner * rows

    def score(j0, i0, deep, wide):
        r = lax.dot_general(
            gathered[1, j0 : j0 + deep, :], gathered[0, i0 : i0 + wide, :], (((1,), (1,)), ((), ())),
            preferred_element_type=F32,
        )
        scores[j0 : j0 + deep, i0 : i0 + wide] = r
        top = jnp.max(r.reshape(deep // 8, 8, wide), axis=0)
        peak[:, i0 : i0 + wide] = jnp.maximum(peak[:, i0 : i0 + wide], top)

    def settle(i0, wide):
        cols = slice(i0, i0 + wide)
        top = jnp.max(peak[:, cols], axis=0, keepdims=True)
        mass[:, cols] = mass[:, cols] * jnp.exp2((shift[0:1, cols] - top) * rate)
        shift[0:1, cols] = top

    strip = 32

    def accumulate(s, i0, cols):
        @pl.loop(0, rows // strip)
        def _(i):
            part = pl.ds(pl.multiple_of(s * rows + i * strip, strip), strip)
            for c in range(i0, i0 + cols, rows):
                lanes = pl.ds(c, rows)
                r = scores[part, lanes]
                e = jnp.exp2((r - shift[0:1, lanes]) * rate)
                hit = lax.broadcasted_iota(jnp.int32, (strip, rows), 0) == pos_all[0:1, lanes] - (base(s) + i * strip)
                g = jnp.where(hit, r, 0.0)
                mass[:, lanes] += jnp.sum(e.reshape(strip // 8, 8, rows), axis=0)
                found[:, lanes] += jnp.sum(g.reshape(strip // 8, 8, rows), axis=0)

    peak[...] = jnp.full(peak.shape, -jnp.inf, F32)
    shift[...] = jnp.full(shift.shape, -jnp.inf, F32)
    mass[...] = jnp.zeros(mass.shape, F32)
    found[...] = jnp.zeros(found.shape, F32)
    score(0, 0, rows, rows)

    for a, d in pairs:
        ag(a, d, 0).wait_recv()
        ag(a, d, 2).start()
        ag(a, d, 3).start()
    for a, d in pairs:
        for k in range(3):
            ag(a, d, k).wait_send()

    @pl.when(first)
    def _():
        pl.semaphore_signal(go_sem, inc=1, device_id=(sibling, me), device_id_type=MESH)

    for copy in metas:
        copy.wait()
    for s in range(SIDE):
        pos_all[:, block(s)] = jnp.broadcast_to(meta[s, 0:1, :], (8, rows)).astype(jnp.int32)
    for a, d in pairs:
        ag(a, d, 1).wait_recv()

    score(rows, 0, 2 * rows, 3 * rows)
    score(0, rows, rows, 2 * rows)
    settle(0, 3 * rows)
    for s in (OWN, NEXT, PREV):
        accumulate(s, 0, 3 * rows)

    for a, d in pairs:
        for k in (2, 3):
            ag(a, d, k).wait_recv()

    score(3 * rows, 0, rows, 2 * rows)
    score(3 * rows, 2 * rows, rows, 2 * rows)
    score(0, 3 * rows, 3 * rows, rows)
    settle(0, total)
    accumulate(FAR, 0, total)
    for s in (OWN, NEXT, PREV):
        accumulate(s, 3 * rows, rows)

    for s in range(SIDE):
        cols = block(s)
        stats[OWN, s] = jnp.zeros(stats.shape[2:], F32)
        stats[OWN, s, 0:1, :] = shift[0:1, cols]
        stats[OWN, s, 1:2, :] = jnp.sum(mass[:, cols], axis=0, keepdims=True)
        stats[OWN, s, 2:3, :] = jnp.sum(found[:, cols], axis=0, keepdims=True)
    posts = [
        remote(stats.at[OWN], stats.at[STEP.index(-STEP[s] % SIDE)], st_send.at[s], st_recv.at[s], at(0, s))
        for s in (NEXT, PREV, FAR)
    ]
    for copy in posts:
        copy.start()
    for copy in posts:
        copy.wait()
    for k in range(SIDE):
        mine = [stats[s, SEEN[s].index(k)] for s in range(SIDE)]
        top = functools.reduce(jnp.maximum, [m[0:1] for m in mine])
        weight = sum(m[1:2] * jnp.exp2((m[0:1] - top) * rate) for m in mine)
        scale = meta[k, 1:2, :] * inv_temp
        shift[0:1, block(k)] = top + (jnp.log2(weight) - jnp.log2(scale)) * (1.0 / rate)
        shift[1:2, block(k)] = scale
        if k == OWN:
            hit = sum(m[2:3] for m in mine)
            loss_ref[...] = ((top - hit) * inv_temp + jnp.log(weight)).reshape(rows)

    def coefficients(s, i0, cols):
        @pl.loop(0, rows // strip)
        def _(i):
            part = pl.ds(pl.multiple_of(s * rows + i * strip, strip), strip)
            for c in range(i0, i0 + cols, rows):
                lanes = pl.ds(c, rows)
                e = jnp.exp2((scores[part, lanes] - shift[0:1, lanes]) * rate)
                hit = lax.broadcasted_iota(jnp.int32, (strip, rows), 0) == pos_all[0:1, lanes] - (base(s) + i * strip)
                coef[part, lanes] = (e - jnp.where(hit, shift[1:2, lanes], 0.0)).astype(BF16)

    def turn(k):
        @pl.loop(0, SIDE)
        def _(s):
            part = pl.ds(pl.multiple_of(s * rows, rows), rows)
            coef_t[k * rows : (k + 1) * rows, part] = coef[part, k * rows : (k + 1) * rows].T

    def product(a, k):
        lhs = coef_t if a == 0 else coef
        return jnp.dot(lhs[k * rows : (k + 1) * rows, :], gathered[1 - a], preferred_element_type=F32)

    def rs(a, d, k):
        h = (d, d, 1 - d, d, d)[k]
        if k < 2:
            rows_of = pl.ds(h * half + k * quarter, quarter)
            src, dst = sent.at[a, 2, rows_of], hop1.at[a, d, pl.ds(k * quarter, quarter)]
        elif k == 2:
            rows_of = pl.ds(h * half, half)
            src, dst = sent.at[a, d, rows_of], hop2.at[a, d, rows_of]
        else:
            rows_of = pl.ds(h * half + (k - 3) * quarter, quarter)
            src, dst = sent.at[a, d, rows_of], hop2.at[a, d, rows_of]
        return remote(src, dst, rs_send.at[a, d, k], rs_recv.at[a, d, k], at(a, (PREV, NEXT)[d]))

    def far(a):
        sent[a, 2] = product(a, FAR).astype(BF16)
        for k in range(2):
            for d in range(2):
                rs(a, d, k).start()

    def near(a, d):
        r = product(a, (PREV, NEXT)[d])
        keep, send = (r[half:], r[:half]) if d == 1 else (r[:half], r[half:])
        partial[a, d] = keep
        sent[a, d, (1 - d) * half : (2 - d) * half, :] = send.astype(BF16)
        rs(a, d, 2).start()

    def own(a):
        (gq_ref, gp_ref)[a][...] = product(a, OWN)

    def pass_on(a, d, k):
        rs(a, d, k).wait_recv()
        rows_of = slice(d * half + k * quarter, d * half + (k + 1) * quarter)
        sent[a, d, rows_of, :] = (
            partial[a, d, k * quarter : (k + 1) * quarter, :]
            + hop1[a, d, k * quarter : (k + 1) * quarter, :].astype(F32)
        ).astype(BF16)
        rs(a, d, k + 3).start()

    coefficients(FAR, 0, total)
    far(1)
    for s in (OWN, NEXT, PREV):
        coefficients(s, 3 * rows, rows)
    turn(FAR)
    far(0)
    for s in (NEXT, PREV, OWN):
        coefficients(s, 0, 3 * rows)
    for d in range(2):
        near(1, d)
    turn(PREV)
    near(0, 0)
    turn(NEXT)
    near(0, 1)
    for k in range(2):
        for a in (1, 0):
            for d in range(2):
                pass_on(a, d, k)
    turn(OWN)
    own(1)
    own(0)

    def add(a, d, k):
        rs(a, d, k).wait_recv()
        out = (gq_ref, gp_ref)[a]
        h = (d, d, 1 - d, d, d)[k]
        start, size = (h * half, half) if k == 2 else (h * half + (k - 3) * quarter, quarter)
        out[start : start + size, :] += hop2[a, d, start : start + size, :].astype(F32)

    for k in (2, 3, 4):
        for a in (1, 0):
            for d in range(2):
                add(a, d, k)

    for a, d in pairs:
        ag(a, d, 3).wait_send()
        for k in range(5):
            rs(a, d, k).wait_send()


def deliver(*refs):
    n = len(refs) // 2
    copies = [pltpu.make_async_copy(refs[i], refs[n + i], refs[-1].at[i]) for i in range(n)]
    for copy in copies:
        copy.start()
    for copy in copies:
        copy.wait()


def per_device(queries, passages, positives, weights):
    rows, width = queries.shape
    total = SIDE * rows
    inv_temp = 2.0 / math.sqrt(width)
    vmem = pl.BlockSpec(memory_space=pltpu.VMEM)
    hbm = pl.BlockSpec(memory_space=pl.ANY)
    dma = pltpu.SemaphoreType.DMA
    results = pl.pallas_call(
        functools.partial(kernel, rows, width, inv_temp),
        out_shape=(
            pltpu.VMEM((rows,), F32),
            pltpu.VMEM((rows, width), F32),
            pltpu.VMEM((rows, width), F32),
        ),
        in_specs=[hbm, hbm, vmem, vmem],
        out_specs=(vmem, vmem, vmem),
        scratch_shapes=[
            pltpu.VMEM((2, rows, width), F32),
            pltpu.VMEM((2, total, width), BF16),
            pltpu.VMEM((total, total), F32),
            pltpu.VMEM((total, total), BF16),
            pltpu.VMEM((total, total), BF16),
            pltpu.VMEM((SIDE, 8, rows), F32),
            pltpu.VMEM((8, total), jnp.int32),
            pltpu.VMEM((SIDE, SIDE, 8, rows), F32),
            pltpu.VMEM((8, total), F32),
            pltpu.VMEM((8, total), F32),
            pltpu.VMEM((8, total), F32),
            pltpu.VMEM((8, total), F32),
            pltpu.VMEM((2, 2, rows // 2, width), F32),
            pltpu.VMEM((2, 3, rows, width), BF16),
            pltpu.VMEM((2, 2, rows // 2, width), BF16),
            pltpu.VMEM((2, 2, rows, width), BF16),
            dma((2,)),
            dma((2, 2, 4)),
            dma((2, 2, 4)),
            dma((SIDE,)),
            dma((SIDE,)),
            dma((SIDE,)),
            dma((SIDE,)),
            dma((2, 2, 5)),
            dma((2, 2, 5)),
            pltpu.SemaphoreType.REGULAR,
        ],
        compiler_params=pltpu.CompilerParams(
            collective_id=0, has_side_effects=True, vmem_limit_bytes=56 * 2**20
        ),
    )(queries, passages, positives, weights)
    return pl.pallas_call(
        deliver,
        out_shape=tuple(jax.ShapeDtypeStruct(r.shape, F32) for r in results),
        in_specs=[hbm] * 3,
        out_specs=(hbm,) * 3,
        scratch_shapes=[dma((3,))],
    )(*[pltpu.with_memory_space_constraint(r, pltpu.VMEM) for r in results])


def solution(mesh):
    split = P(("dp", "group"))
    whole = P(("dp", "group"), None)
    return jax.shard_map(
        per_device,
        mesh=mesh,
        in_specs=(whole, whole, split, split),
        out_specs=(split, whole, whole),
        check_vma=False,
    )
```

time: 97.4 us -> 74.5 us (0.76)
  Pallas kernels: 88.8 us -> 73.5 us
  local copies, waits for them, and re-layouts: 6.48 us -> 0 us
  other arithmetic: 1.27 us -> 0 us
    pallas_call x1, Pallas kernels: 88.8 us -> 71.8 us  [per_device(): pl.pallas_call(functools.partial(kernel, rows, width, inv_temp), out_shap...]
    unnamed x4 -> x0, local copies, waits for them, and re-layouts: 3.99 us -> none
    reshape x2 -> x0, local copies, waits for them, and re-layouts: 2.49 us -> none  [the longest x1 1.25 us: per_device(): positives.reshape(1, rows)]
    pallas_call x0 -> x1, Pallas kernels: none -> 1.69 us  [per_device(): pl.pallas_call(deliver, out_shape=tuple((jax.ShapeDtypeStruct(r.shape, F3...]
    pallas_call x1 -> x0, other arithmetic: 1.27 us -> none  [per_device(): pl.pallas_call(functools.partial(kernel, rows, width, inv_temp), out_shap...]
where the time goes in v2:
time: 74.5 us; the launch traced here: 74.3 us
  Pallas kernels  73.5 us (99%)
  between operations  0.8 us (1%)
    pallas_call x1, Pallas kernels, per_device(): pl.pallas_call(functools.partial(kernel, rows, width, inv_temp), out_shap...  71.8 us
    pallas_call x1, Pallas kernels, per_device(): pl.pallas_call(deliver, out_shape=tuple((jax.ShapeDtypeStruct(r.shape, F3...  1.69 us

profile of v2, /device:TPU:1, one launch (start us, length us, event | category | flops | bytes accessed | tf_op | source)
XLA Modules:
  0.0 74.3 jit_solution(10294088764635512330)
XLA Ops:
  0.6 71.8 %shard_map.67 = (f32[384]{0:T(512)S(1)}, f32[384,1024]{1,0:T(8,128)S(1)}, f32[384,1024]{1,0:T(8,128)S(1)}) custom-call(f32[384,1024]{1,0:T(8,128)} %q_hbm.1, f32[384,1024]{1,0:T(8,128)} %p_hbm.1, s32[384]{0:T(512)} %pos_ref.1, f32[384]{0:T(512)} %w_ref.1), custom_call_target="tpu_custom_call" | custom-call | tf_op jit(solution)/shard_map/pallas_call | solution.py:317
  72.5 1.7 %shard_map.68 = (f32[384]{0:T(512)}, f32[384,1024]{1,0:T(8,128)}, f32[384,1024]{1,0:T(8,128)}) custom-call(f32[384]{0:T(512)S(1)} %get-tuple-element.6.refs_0_, f32[384,1024]{1,0:T(8,128)S(1)} %get-tuple-element.7.refs_1_, f32[384,1024]{1,0:T(8,128)S(1)} %get-tuple-element.8.refs_2_), custom_call_target="tpu_custom_call" | custom-call | tf_op jit(solution)/shard_map/pallas_call | solution.py:358

commit v3 on v2

v3 whole, which is shorter than its diff:
```python
import functools
import math

import jax
import jax.numpy as jnp
from jax import lax
from jax.experimental import pallas as pl
from jax.experimental.pallas import tpu as pltpu
from jax.sharding import PartitionSpec as P

MESH = pl.DeviceIdType.MESH
SIDE = 4
OWN, NEXT, PREV, FAR = range(4)
STEP = (0, 1, 3, 2)
SEEN = tuple(tuple(STEP.index((STEP[s] + STEP[k]) % SIDE) for k in range(SIDE)) for s in range(SIDE))
LOG2E = math.log2(math.e)
BF16, F32 = jnp.bfloat16, jnp.float32


def kernel(
    rows, width, inv_temp,
    q_hbm, p_hbm, pos_ref, w_ref,
    loss_ref, gq_ref, gp_ref,
    stage, gathered, scores, coef, meta, pos_all, stats, peak, mass, found, shift, sent, hop1, hop2,
    load_sem, ag_send, ag_recv, meta_send, meta_recv, st_send, st_recv, rs_send, rs_recv, go_sem,
):
    half, quarter = rows // 2, rows // 4
    total = SIDE * rows
    rate = inv_temp * LOG2E
    dp, me = lax.axis_index("dp"), lax.axis_index("group")
    z, y = me // SIDE, me % SIDE
    first = dp % 2 == 0
    sibling = dp + 1 - 2 * (dp % 2)

    def at(axis, slot):
        if axis == 0:
            return (dp, z * SIDE + (y + STEP[slot]) % SIDE)
        return (dp, (z + STEP[slot]) % SIDE * SIDE + y)

    greet = [at(0, NEXT), at(0, PREV), at(0, FAR), at(1, NEXT), at(1, PREV), (sibling, me)]
    barrier = pltpu.get_barrier_semaphore()
    for device in greet:
        pl.semaphore_signal(barrier, inc=1, device_id=device, device_id_type=MESH)

    def load(a, n):
        part = pl.ds(n * quarter, quarter)
        return pltpu.make_async_copy((q_hbm, p_hbm)[a].at[part], stage.at[a, part], load_sem.at[a, n])

    order = [(a, d, k) for k in range(2) for d in range(2) for a in (1, 0)]
    for a, d, k in order:
        load(a, 2 * d + k).start()
    meta[OWN] = jnp.zeros(meta.shape[1:], F32)
    meta[OWN, 0:1, :] = pos_ref[...].reshape(1, rows).astype(F32)
    meta[OWN, 1:2, :] = w_ref[...].reshape(1, rows)

    def block(slot):
        return pl.ds(slot * rows, rows)

    def remote(src, dst, send, recv, device):
        return pltpu.make_async_remote_copy(
            src_ref=src, dst_ref=dst, send_sem=send, recv_sem=recv, device_id=device, device_id_type=MESH
        )

    metas = [
        remote(meta.at[OWN], meta.at[STEP.index(-STEP[s] % SIDE)], meta_send.at[s], meta_recv.at[s], at(0, s))
        for s in (NEXT, PREV, FAR)
    ]
    def ag(a, d, k):
        near = (NEXT, PREV)[d]
        start, size = ((1 - d) * half, half) if k == 2 else (d * half + k % 3 * quarter, quarter)
        src, dst = (OWN, near) if k < 3 else (near, FAR)
        src, dst = (pl.ds(slot * rows + start, size) for slot in (src, dst))
        return remote(
            gathered.at[a, src], gathered.at[a, dst],
            ag_send.at[a, d, k], ag_recv.at[a, d, k], at(a, (PREV, NEXT)[d]),
        )

    pairs = [(a, d) for d in range(2) for a in (1, 0)]

    def cast(a, n):
        load(a, n).wait()

        @pl.loop(0, quarter // 16)
        def _(i):
            part = pl.ds(pl.multiple_of(n * quarter + i * 16, 16), 16)
            gathered[a, part, :] = stage[a, part, :].astype(BF16)

    @pl.when(first)
    def _():
        for n, (a, d, k) in enumerate(order):
            cast(a, 2 * d + k)
            if n == 0:
                pl.semaphore_wait(barrier, len(greet))
            ag(a, d, k).start()
        for a, d in pairs:
            ag(a, d, 2).start()
        for copy in metas:
            copy.start()

    @pl.when(jnp.logical_not(first))
    def _():
        for a, d, k in order:
            cast(a, 2 * d + k)
        pl.semaphore_wait(barrier, len(greet))
        for copy in metas:
            copy.start()
        pl.semaphore_wait(go_sem, 1)
        for k in range(3):
            for a, d in pairs:
                ag(a, d, k).start()

    def base(slot):
        owner = (z + STEP[slot]) % SIDE * SIDE + y
        return owner * rows

    def score(j0, i0, deep, wide):
        r = lax.dot_general(
            gathered[1, j0 : j0 + deep, :], gathered[0, i0 : i0 + wide, :], (((1,), (1,)), ((), ())),
            preferred_element_type=F32,
        )
        scores[j0 : j0 + deep, i0 : i0 + wide] = r
        top = jnp.max(r.reshape(deep // 8, 8, wide), axis=0)
        peak[:, i0 : i0 + wide] = jnp.maximum(peak[:, i0 : i0 + wide], top)

    def settle(i0, wide):
        cols = slice(i0, i0 + wide)
        top = jnp.max(peak[:, cols], axis=0, keepdims=True)
        mass[:, cols] = mass[:, cols] * jnp.exp2((shift[0:1, cols] - top) * rate)
        shift[0:1, cols] = top

    strip = 64 if rows % 64 == 0 else rows

    def accumulate(s, i0, cols):
        @pl.loop(0, rows // strip)
        def _(i):
            part = pl.ds(pl.multiple_of(s * rows + i * strip, strip), strip)
            for c in range(i0, i0 + cols, rows):
                lanes = pl.ds(c, rows)
                r = scores[part, lanes]
                e = jnp.exp2((r - shift[0:1, lanes]) * rate)
                scores[part, lanes] = e
                hit = lax.broadcasted_iota(jnp.int32, (strip, rows), 0) == pos_all[0:1, lanes] - (base(s) + i * strip)
                g = jnp.where(hit, r, 0.0)
                mass[:, lanes] += jnp.sum(e.reshape(strip // 8, 8, rows), axis=0)
                found[:, lanes] += jnp.sum(g.reshape(strip // 8, 8, rows), axis=0)

    peak[...] = jnp.full(peak.shape, -jnp.inf, F32)
    shift[...] = jnp.full(shift.shape, -jnp.inf, F32)
    mass[...] = jnp.zeros(mass.shape, F32)
    found[...] = jnp.zeros(found.shape, F32)
    score(0, 0, rows, rows)

    for k in range(2):
        for a, d in pairs:
            ag(a, d, k).wait_recv()
            ag(a, d, k + 3).start()
    for a, d in pairs:
        for k in range(4):
            ag(a, d, k).wait_send()

    @pl.when(first)
    def _():
        pl.semaphore_signal(go_sem, inc=1, device_id=(sibling, me), device_id_type=MESH)

    for copy in metas:
        copy.wait()
    for s in range(SIDE):
        pos_all[:, block(s)] = jnp.broadcast_to(meta[s, 0:1, :], (8, rows)).astype(jnp.int32)
    for a, d in pairs:
        ag(a, d, 2).wait_recv()

    score(rows, 0, 2 * rows, 3 * rows)
    score(0, rows, rows, 2 * rows)
    settle(0, 3 * rows)
    for s in (OWN, NEXT, PREV):
        accumulate(s, 0, 3 * rows)

    for a, d in pairs:
        for k in (3, 4):
            ag(a, d, k).wait_recv()

    score(3 * rows, 0, rows, 2 * rows)
    score(3 * rows, 2 * rows, rows, 2 * rows)
    score(0, 3 * rows, 3 * rows, rows)
    shift[1:2, :] = shift[0:1, :]
    settle(0, total)
    accumulate(FAR, 0, total)
    for s in (OWN, NEXT, PREV):
        accumulate(s, 3 * rows, rows)

    for s in range(SIDE):
        cols = block(s)
        stats[OWN, 0, s : s + 1, :] = shift[0:1, cols]
        stats[OWN, 0, SIDE + s : SIDE + s + 1, :] = jnp.sum(mass[:, cols], axis=0, keepdims=True)
        stats[OWN, 1, s : s + 1, :] = jnp.sum(found[:, cols], axis=0, keepdims=True)
    posts, late_posts = (
        [
            remote(stats.at[OWN, n], stats.at[STEP.index(-STEP[s] % SIDE), n], st_send.at[n, s], st_recv.at[n, s], at(0, s))
            for s in (NEXT, PREV, FAR)
        ]
        for n in range(2)
    )
    for copy in posts + late_posts:
        copy.start()

    def product(a, k, start, size, part=None):
        rhs = gathered[1 - a, :, start : start + size]
        if a == 0:
            lhs = coef[:, k * rows : (k + 1) * rows]
            return lax.dot_general(lhs, rhs, (((0,), (0,)), ((), ())), preferred_element_type=F32)
        first_row, end = part or (0, rows)
        return jnp.dot(coef[k * rows + first_row : k * rows + end, :], rhs, preferred_element_type=F32)

    for s in range(SIDE):

        @pl.loop(0, rows // strip)
        def _(i):
            part = pl.ds(pl.multiple_of(s * rows + i * strip, strip), strip)
            coef[part, block(FAR)] = scores[part, block(FAR)].astype(BF16)
            hit = lax.broadcasted_iota(jnp.int32, (strip, rows), 0) == pos_all[0:1, block(FAR)] - (base(s) + i * strip)
            coef[part, block(OWN)] = jnp.where(hit, 1.0, 0.0).astype(BF16)

    stage[0] = product(0, FAR, 0, width)
    stage[1] = product(0, OWN, 0, width)

    for copy in posts:
        copy.wait()
    for k in range(SIDE):
        mine = [stats[s, 0] for s in range(SIDE)]
        places = [SEEN[s].index(k) for s in range(SIDE)]
        tops = [m[p : p + 1] for m, p in zip(mine, places)]
        top = functools.reduce(jnp.maximum, tops)
        weight = sum(
            m[SIDE + p : SIDE + p + 1] * jnp.exp2((t - top) * rate) for m, p, t in zip(mine, places, tops)
        )
        scale = meta[k, 1:2, :] * inv_temp
        for n in range(2):
            shift[2 + n : 3 + n, block(k)] = jnp.exp2((shift[n : n + 1, block(k)] - top) * rate) * (scale / weight)
        shift[4:5, block(k)] = scale
        if k == OWN:
            peak[0:1, block(OWN)] = top * inv_temp + jnp.log(weight)

    def coefficients(s, i0, cols):
        n = 0 if s == FAR or i0 == 3 * rows else 1

        @pl.loop(0, rows // strip)
        def _(i):
            part = pl.ds(pl.multiple_of(s * rows + i * strip, strip), strip)
            for c in range(i0, i0 + cols, rows):
                lanes = pl.ds(c, rows)
                e = scores[part, lanes] * shift[2 + n : 3 + n, lanes]
                hit = lax.broadcasted_iota(jnp.int32, (strip, rows), 0) == pos_all[0:1, lanes] - (base(s) + i * strip)
                coef[part, lanes] = (e - jnp.where(hit, shift[4:5, lanes], 0.0)).astype(BF16)

    side = width // 2

    def rs(a, d, k):
        rows_of = pl.ds((k if k < 2 else k - 3) * half, half)
        if k < 2:
            src, dst = sent.at[a, 2, d, rows_of], hop1.at[a, d, rows_of]
        elif k == 2:
            src, dst = sent.at[a, d, 1 - d], hop2.at[a, d, 1 - d]
        else:
            src, dst = sent.at[a, d, d, rows_of], hop2.at[a, d, d, rows_of]
        return remote(src, dst, rs_send.at[a, d, k], rs_recv.at[a, d, k], at(a, (PREV, NEXT)[d]))

    def far_passages(d, k):
        part = slice(k * half, (k + 1) * half)
        sent[1, 2, d, part, :] = product(1, FAR, d * side, side, (k * half, (k + 1) * half)).astype(BF16)
        rs(1, d, k).start()

    def far_queries():
        factors = shift[:, block(FAR)].T
        for d in range(2):
            cols = slice(d * side, (d + 1) * side)
            sent[0, 2, d] = (stage[0, :, cols] * factors[:, 2:3] - stage[1, :, cols] * factors[:, 4:5]).astype(BF16)
            for k in range(2):
                rs(0, d, k).start()

    def near(a, d):
        sent[a, d, 1 - d] = product(a, (PREV, NEXT)[d], (1 - d) * side, side).astype(BF16)
        rs(a, d, 2).start()

    def pass_on(a, d):
        r = product(a, (PREV, NEXT)[d], d * side, side)
        for k in range(2):
            rs(a, d, k).wait_recv()
            part = slice(k * half, (k + 1) * half)
            sent[a, d, d, part, :] = (r[part] + hop1[a, d, part, :].astype(F32)).astype(BF16)
            rs(a, d, k + 3).start()

    coefficients(FAR, 0, total)
    for d in range(2):
        far_passages(d, 0)
    far_queries()
    for d in range(2):
        far_passages(d, 1)
    for s in (NEXT, PREV, OWN):
        coefficients(s, 3 * rows, rows)
        coefficients(s, 0, 3 * rows)
    for a in (1, 0):
        for d in range(2):
            near(a, d)
    for a in (1, 0):
        for d in range(2):
            pass_on(a, d)
    for a in (1, 0):
        (gq_ref, gp_ref)[a][...] = product(a, OWN, 0, width)
    for copy in late_posts:
        copy.wait()
    hit = sum(stats[s, 1, SEEN[s].index(OWN) : SEEN[s].index(OWN) + 1, :] for s in range(SIDE))
    loss_ref[...] = (peak[0:1, block(OWN)] - hit * inv_temp).reshape(rows)

    def add(a, d, k):
        rs(a, d, k).wait_recv()
        out = (gq_ref, gp_ref)[a]
        h = 1 - d if k == 2 else d
        part = slice(0, rows) if k == 2 else slice((k - 3) * half, (k - 2) * half)
        out[part, h * side : (h + 1) * side] += hop2[a, d, h, part, :].astype(F32)

    for k in (2, 3, 4):
        for a in (1, 0):
            for d in range(2):
                add(a, d, k)

    for a, d in pairs:
        ag(a, d, 4).wait_send()
        for k in range(5):
            rs(a, d, k).wait_send()


def deliver(*refs):
    n = len(refs) // 2
    copies = [pltpu.make_async_copy(refs[i], refs[n + i], refs[-1].at[i]) for i in range(n)]
    for copy in copies:
        copy.start()
    for copy in copies:
        copy.wait()


def per_device(queries, passages, positives, weights):
    rows, width = queries.shape
    total = SIDE * rows
    inv_temp = 2.0 / math.sqrt(width)
    vmem = pl.BlockSpec(memory_space=pltpu.VMEM)
    hbm = pl.BlockSpec(memory_space=pl.ANY)
    dma = pltpu.SemaphoreType.DMA
    results = pl.pallas_call(
        functools.partial(kernel, rows, width, inv_temp),
        out_shape=(
            pltpu.VMEM((rows,), F32),
            pltpu.VMEM((rows, width), F32),
            pltpu.VMEM((rows, width), F32),
        ),
        in_specs=[hbm, hbm, vmem, vmem],
        out_specs=(vmem, vmem, vmem),
        scratch_shapes=[
            pltpu.VMEM((2, rows, width), F32),
            pltpu.VMEM((2, total, width), BF16),
            pltpu.VMEM((total, total), F32),
            pltpu.VMEM((total, total), BF16),
            pltpu.VMEM((SIDE, 8, rows), F32),
            pltpu.VMEM((8, total), jnp.int32),
            pltpu.VMEM((SIDE, 2, 2 * SIDE, rows), F32),
            pltpu.VMEM((8, total), F32),
            pltpu.VMEM((8, total), F32),
            pltpu.VMEM((8, total), F32),
            pltpu.VMEM((8, total), F32),
            pltpu.VMEM((2, 3, 2, rows, width // 2), BF16),
            pltpu.VMEM((2, 2, rows, width // 2), BF16),
            pltpu.VMEM((2, 2, 2, rows, width // 2), BF16),
            dma((2, 4)),
            dma((2, 2, 5)),
            dma((2, 2, 5)),
            dma((SIDE,)),
            dma((SIDE,)),
            dma((2, SIDE)),
            dma((2, SIDE)),
            dma((2, 2, 5)),
            dma((2, 2, 5)),
            pltpu.SemaphoreType.REGULAR,
        ],
        compiler_params=pltpu.CompilerParams(
            collective_id=0, has_side_effects=True, vmem_limit_bytes=56 * 2**20
        ),
    )(queries, passages, positives, weights)
    return pl.pallas_call(
        deliver,
        out_shape=tuple(jax.ShapeDtypeStruct(r.shape, F32) for r in results),
        in_specs=[hbm] * 3,
        out_specs=(hbm,) * 3,
        scratch_shapes=[dma((3,))],
    )(*[pltpu.with_memory_space_constraint(r, pltpu.VMEM) for r in results])


def solution(mesh):
    split = P(("dp", "group"))
    whole = P(("dp", "group"), None)
    return jax.shard_map(
        per_device,
        mesh=mesh,
        in_specs=(whole, whole, split, split),
        out_specs=(split, whole, whole),
        check_vma=False,
    )
```

time: 74.5 us -> 68.5 us (0.919)
  Pallas kernels: 73.5 us -> 67.6 us
    pallas_call x1, Pallas kernels: 71.8 us -> 65.9 us  [per_device(): pl.pallas_call(functools.partial(kernel, rows, width, inv_temp), out_shap...]
where the time goes in v3:
time: 68.5 us; the launch traced here: 68.4 us
  Pallas kernels  67.6 us (99%)
  between operations  0.8 us (1%)
    pallas_call x1, Pallas kernels, per_device(): pl.pallas_call(functools.partial(kernel, rows, width, inv_temp), out_shap...  65.9 us
    pallas_call x1, Pallas kernels, per_device(): pl.pallas_call(deliver, out_shape=tuple((jax.ShapeDtypeStruct(r.shape, F3...  1.69 us

profile of v3, /device:TPU:1, one launch (start us, length us, event | category | flops | bytes accessed | tf_op | source)
XLA Modules:
  0.0 68.4 jit_solution(15342535935852586249)
XLA Ops:
  0.6 65.9 %shard_map.67 = (f32[384]{0:T(512)S(1)}, f32[384,1024]{1,0:T(8,128)S(1)}, f32[384,1024]{1,0:T(8,128)S(1)}) custom-call(f32[384,1024]{1,0:T(8,128)} %q_hbm.1, f32[384,1024]{1,0:T(8,128)} %p_hbm.1, s32[384]{0:T(512)} %pos_ref.1, f32[384]{0:T(512)} %w_ref.1), custom_call_target="tpu_custom_call" | custom-call | tf_op jit(solution)/shard_map/pallas_call | solution.py:348
  66.5 1.7 %shard_map.68 = (f32[384]{0:T(512)}, f32[384,1024]{1,0:T(8,128)}, f32[384,1024]{1,0:T(8,128)}) custom-call(f32[384]{0:T(512)S(1)} %get-tuple-element.6.refs_0_, f32[384,1024]{1,0:T(8,128)S(1)} %get-tuple-element.7.refs_1_, f32[384,1024]{1,0:T(8,128)S(1)} %get-tuple-element.8.refs_2_), custom_call_target="tpu_custom_call" | custom-call | tf_op jit(solution)/shard_map/pallas_call | solution.py:387

commit v4 on v3

--- a/solution.py
+++ b/solution.py
@@ -21,7 +21,7 @@
     rows, width, inv_temp,
     q_hbm, p_hbm, pos_ref, w_ref,
     loss_ref, gq_ref, gp_ref,
-    stage, gathered, scores, coef, meta, pos_all, stats, peak, mass, found, shift, sent, hop1, hop2,
+    stage, gathered, scores, terms, coef, meta, pos_all, stats, peak, mass, found, shift, sent, hop1, hop2,
     load_sem, ag_send, ag_recv, meta_send, meta_recv, st_send, st_recv, rs_send, rs_recv, go_sem,
 ):
     half, quarter = rows // 2, rows // 4
@@ -91,11 +91,11 @@
             cast(a, 2 * d + k)
             if n == 0:
                 pl.semaphore_wait(barrier, len(greet))
+                for copy in metas:
+                    copy.start()
             ag(a, d, k).start()
         for a, d in pairs:
             ag(a, d, 2).start()
-        for copy in metas:
-            copy.start()
 
     @pl.when(jnp.logical_not(first))
     def _():
@@ -138,11 +138,35 @@
                 lanes = pl.ds(c, rows)
                 r = scores[part, lanes]
                 e = jnp.exp2((r - shift[0:1, lanes]) * rate)
-                scores[part, lanes] = e
-                hit = lax.broadcasted_iota(jnp.int32, (strip, rows), 0) == pos_all[0:1, lanes] - (base(s) + i * strip)
-                g = jnp.where(hit, r, 0.0)
+                terms[part, lanes] = e
+                if c == 3 * rows:
+                    coef[part, lanes] = e.astype(BF16)
                 mass[:, lanes] += jnp.sum(e.reshape(strip // 8, 8, rows), axis=0)
-                found[:, lanes] += jnp.sum(g.reshape(strip // 8, 8, rows), axis=0)
+
+    def seek():
+        for s in range(SIDE):
+
+            @pl.loop(0, rows // strip)
+            def _(i):
+                part = pl.ds(pl.multiple_of(s * rows + i * strip, strip), strip)
+                for c in range(0, total, rows):
+                    lanes = pl.ds(c, rows)
+                    hit = lax.broadcasted_iota(jnp.int32, (strip, rows), 0) == pos_all[0:1, lanes] - (base(s) + i * strip)
+                    g = jnp.where(hit, scores[part, lanes], 0.0)
+                    found[:, lanes] += jnp.sum(g.reshape(strip // 8, 8, rows), axis=0)
+
+        for s in range(SIDE):
+            stats[OWN, 1, s : s + 1, :] = jnp.sum(found[:, block(s)], axis=0, keepdims=True)
+        for copy in late_posts:
+            copy.start()
+
+    def product(a, k, start, size, part=None):
+        rhs = gathered[1 - a, :, start : start + size]
+        if a == 0:
+            lhs = coef[:, k * rows : (k + 1) * rows]
+            return lax.dot_general(lhs, rhs, (((0,), (0,)), ((), ())), preferred_element_type=F32)
+        first_row, end = part or (0, rows)
+        return jnp.dot(coef[k * rows + first_row : k * rows + end, :], rhs, preferred_element_type=F32)
 
     peak[...] = jnp.full(peak.shape, -jnp.inf, F32)
     shift[...] = jnp.full(shift.shape, -jnp.inf, F32)
@@ -166,6 +190,22 @@
         copy.wait()
     for s in range(SIDE):
         pos_all[:, block(s)] = jnp.broadcast_to(meta[s, 0:1, :], (8, rows)).astype(jnp.int32)
+
+    for s in range(SIDE):
+
+        @pl.loop(0, rows // strip)
+        def _(i):
+            part = pl.ds(pl.multiple_of(s * rows + i * strip, strip), strip)
+            hit = lax.broadcasted_iota(jnp.int32, (strip, rows), 0) == pos_all[0:1, block(FAR)] - (base(s) + i * strip)
+            coef[part, block(OWN)] = jnp.where(hit, 1.0, 0.0).astype(BF16)
+
+    def hits(start, end):
+        return lax.dot_general(
+            coef[start:end, block(OWN)], gathered[1, start:end, :], (((0,), (0,)), ((), ())), preferred_element_type=F32
+        )
+
+    early = rows + (rows // 3 if rows % 3 == 0 else rows // 2)
+    stage[1] = hits(0, early)
     for a, d in pairs:
         ag(a, d, 2).wait_recv()
 
@@ -192,7 +232,6 @@
         cols = block(s)
         stats[OWN, 0, s : s + 1, :] = shift[0:1, cols]
         stats[OWN, 0, SIDE + s : SIDE + s + 1, :] = jnp.sum(mass[:, cols], axis=0, keepdims=True)
-        stats[OWN, 1, s : s + 1, :] = jnp.sum(found[:, cols], axis=0, keepdims=True)
     posts, late_posts = (
         [
             remote(stats.at[OWN, n], stats.at[STEP.index(-STEP[s] % SIDE), n], st_send.at[n, s], st_recv.at[n, s], at(0, s))
@@ -200,28 +239,12 @@
         ]
         for n in range(2)
     )
-    for copy in posts + late_posts:
+    for copy in posts:
         copy.start()
 
-    def product(a, k, start, size, part=None):
-        rhs = gathered[1 - a, :, start : start + size]
-        if a == 0:
-            lhs = coef[:, k * rows : (k + 1) * rows]
-            return lax.dot_general(lhs, rhs, (((0,), (0,)), ((), ())), preferred_element_type=F32)
-        first_row, end = part or (0, rows)
-        return jnp.dot(coef[k * rows + first_row : k * rows + end, :], rhs, preferred_element_type=F32)
-
-    for s in range(SIDE):
-
-        @pl.loop(0, rows // strip)
-        def _(i):
-            part = pl.ds(pl.multiple_of(s * rows + i * strip, strip), strip)
-            coef[part, block(FAR)] = scores[part, block(FAR)].astype(BF16)
-            hit = lax.broadcasted_iota(jnp.int32, (strip, rows), 0) == pos_all[0:1, block(FAR)] - (base(s) + i * strip)
-            coef[part, block(OWN)] = jnp.where(hit, 1.0, 0.0).astype(BF16)
-
     stage[0] = product(0, FAR, 0, width)
-    stage[1] = product(0, OWN, 0, width)
+    stage[1] = stage[1] + hits(early, total)
+    seek()
 
     for copy in posts:
         copy.wait()
@@ -248,7 +271,7 @@
             part = pl.ds(pl.multiple_of(s * rows + i * strip, strip), strip)
             for c in range(i0, i0 + cols, rows):
                 lanes = pl.ds(c, rows)
-                e = scores[part, lanes] * shift[2 + n : 3 + n, lanes]
+                e = terms[part, lanes] * shift[2 + n : 3 + n, lanes]
                 hit = lax.broadcasted_iota(jnp.int32, (strip, rows), 0) == pos_all[0:1, lanes] - (base(s) + i * strip)
                 coef[part, lanes] = (e - jnp.where(hit, shift[4:5, lanes], 0.0)).astype(BF16)
 
@@ -264,10 +287,13 @@
             src, dst = sent.at[a, d, d, rows_of], hop2.at[a, d, d, rows_of]
         return remote(src, dst, rs_send.at[a, d, k], rs_recv.at[a, d, k], at(a, (PREV, NEXT)[d]))
 
-    def far_passages(d, k):
+    def far_passages(k):
         part = slice(k * half, (k + 1) * half)
-        sent[1, 2, d, part, :] = product(1, FAR, d * side, side, (k * half, (k + 1) * half)).astype(BF16)
-        rs(1, d, k).start()
+        r = product(1, FAR, 0, width, (k * half, (k + 1) * half)).astype(BF16)
+        for d in range(2):
+            sent[1, 2, d, part, :] = r[:, d * side : (d + 1) * side]
+        for d in range(2):
+            rs(1, d, k).start()
 
     def far_queries():
         factors = shift[:, block(FAR)].T
@@ -290,11 +316,9 @@
             rs(a, d, k + 3).start()
 
     coefficients(FAR, 0, total)
-    for d in range(2):
-        far_passages(d, 0)
+    far_passages(0)
     far_queries()
-    for d in range(2):
-        far_passages(d, 1)
+    far_passages(1)
     for s in (NEXT, PREV, OWN):
         coefficients(s, 3 * rows, rows)
         coefficients(s, 0, 3 * rows)
@@ -357,6 +381,7 @@
         scratch_shapes=[
             pltpu.VMEM((2, rows, width), F32),
             pltpu.VMEM((2, total, width), BF16),
+            pltpu.VMEM((total, total), F32),
             pltpu.VMEM((total, total), F32),
             pltpu.VMEM((total, total), BF16),
             pltpu.VMEM((SIDE, 8, rows), F32),

time: 68.5 us -> 67.6 us (0.987)
  Pallas kernels: 67.6 us -> 66.7 us
    pallas_call x1, Pallas kernels: 65.9 us -> 65 us  [per_device(): pl.pallas_call(functools.partial(kernel, rows, width, inv_temp), out_shap...]
where the time goes in v4:
time: 67.6 us; the launch traced here: 67.5 us
  Pallas kernels  66.7 us (99%)
  between operations  0.8 us (1%)
    pallas_call x1, Pallas kernels, per_device(): pl.pallas_call(functools.partial(kernel, rows, width, inv_temp), out_shap...  65 us
    pallas_call x1, Pallas kernels, per_device(): pl.pallas_call(deliver, out_shape=tuple((jax.ShapeDtypeStruct(r.shape, F3...  1.69 us

profile of v4, /device:TPU:1, one launch (start us, length us, event | category | flops | bytes accessed | tf_op | source)
XLA Modules:
  0.0 67.5 jit_solution(164192626034480081)
XLA Ops:
  0.6 65.0 %shard_map.67 = (f32[384]{0:T(512)S(1)}, f32[384,1024]{1,0:T(8,128)S(1)}, f32[384,1024]{1,0:T(8,128)S(1)}) custom-call(f32[384,1024]{1,0:T(8,128)} %q_hbm.1, f32[384,1024]{1,0:T(8,128)} %p_hbm.1, s32[384]{0:T(512)} %pos_ref.1, f32[384]{0:T(512)} %w_ref.1), custom_call_target="tpu_custom_call" | custom-call | tf_op jit(solution)/shard_map/pallas_call | solution.py:372
  65.7 1.7 %shard_map.68 = (f32[384]{0:T(512)}, f32[384,1024]{1,0:T(8,128)}, f32[384,1024]{1,0:T(8,128)}) custom-call(f32[384]{0:T(512)S(1)} %get-tuple-element.6.refs_0_, f32[384,1024]{1,0:T(8,128)S(1)} %get-tuple-element.7.refs_1_, f32[384,1024]{1,0:T(8,128)S(1)} %get-tuple-element.8.refs_2_), custom_call_target="tpu_custom_call" | custom-call | tf_op jit(solution)/shard_map/pallas_call | solution.py:412
